TPU v7x, 32 devices: a whole 2x2x4 slice. The times are simulated.
32 devices in a mesh: ctx: 16 (over z, y, x), head: 2 (over core).
Axes of the slice: x: 2, y: 2, z: 4, core: 2. Of those that a mesh axis runs over, the one named last changes fastest.
Arguments:
- query_rows: float32 [4096, 4096], P('ctx', 'head'), may hold values from -6 to 6
- key_rows: float32 [2, 4096, 4096], P(None, 'ctx', 'head'), may hold values from -8 to 8
- reflection_value_rows: float32 [2, 4096, 4096], P(None, 'ctx', 'head'), may hold values from -6 to 6
- beta_logit: float32 [2, 32, 4096], P(None, 'head', 'ctx'), may hold values from -8 to 8
Outputs:
- normed: float32 [4096, 4096], P('ctx', 'head')
All inputs are finite; a program needn't handle non-finite values.
Results may differ from a plain program's by a relative error of at most 0.00013.
Values sent between devices are 32-bit elements; how exact they have to be, the bound alone decides.
A program may use at most 128 MiB of HBM per device.

v0:
```python
import jax
import jax.numpy as jnp
from jax import lax
from jax.sharding import PartitionSpec as P

HEADS = 32
DK = 128
DV = 128
GROUP = 64


highest_mode = lax.Precision.HIGHEST


def from_behind(value, axis, steps):
    count = lax.axis_size(axis)
    initial, last = (max(0, -steps), min(count, count - steps))
    return lax.ppermute(value, axis, [(source, source + steps) for source in range(initial, last)])


def matmul_hi(left, right):
    return jnp.einsum("...ij,...jk->...ik", left, right, precision=highest_mode)


def unit_rows(matrix):
    return matrix * lax.rsqrt(jnp.sum(matrix * matrix, axis=-1, keepdims=True) + 1e-06)


def group_terms(query_blk, key_blk, value_blk, gate_strength_slab):
    width_v = value_blk.shape[-1]
    width_k = key_blk.shape[-1]
    steps_n = key_blk.shape[-2]
    rows_n = query_blk.shape[-2]
    key_gram = jnp.einsum("...id,...jd->...ij", key_blk, key_blk, precision=highest_mode)
    row_index = lax.broadcasted_iota(jnp.int32, (steps_n, steps_n), 0)
    col_index = lax.broadcasted_iota(jnp.int32, (steps_n, steps_n), 1)
    strict = row_index > col_index
    unit_lower = jnp.eye(steps_n, dtype=jnp.float32) + jnp.where(
        strict, gate_strength_slab[..., :, None] * key_gram, 0.0
    )
    right_cols = gate_strength_slab[..., :, None] * jnp.concatenate([value_blk, key_blk], axis=-1)
    solved = jax.scipy.linalg.solve_triangular(
        unit_lower, right_cols, lower=True, unit_diagonal=True
    )
    fresh_values = solved[..., :width_v]
    wy_keys = solved[..., width_v:]
    transition = jnp.eye(width_k, dtype=jnp.float32) - jnp.einsum(
        "...id,...ie->...de", key_blk, wy_keys, precision=highest_mode
    )
    pushed = jnp.einsum("...id,...ie->...de", key_blk, fresh_values, precision=highest_mode)
    scores = jnp.einsum("...td,...id->...ti", query_blk, key_blk, precision=highest_mode)
    token_index = lax.broadcasted_iota(jnp.int32, (rows_n, steps_n), 0)
    sub_index = lax.broadcasted_iota(jnp.int32, (rows_n, steps_n), 1)
    causal_visible = sub_index // 2 <= token_index
    masked = jnp.where(causal_visible, scores, 0.0)
    query_eff = query_blk - matmul_hi(masked, wy_keys)
    inner_portion = matmul_hi(masked, fresh_values)
    return (transition, pushed, query_eff, inner_portion)


def local(query_rows, key_rows, reflection_value_rows, beta_logit):
    tok_local = query_rows.shape[0]
    heads_here = query_rows.shape[1] // DK
    groups = tok_local // GROUP
    query_blk = unit_rows(query_rows.reshape(groups, GROUP, heads_here, DK)).transpose(0, 2, 1, 3)
    key_blk = (
        unit_rows(key_rows.reshape(2, groups, GROUP, heads_here, DK))
        .transpose(1, 3, 2, 0, 4)
        .reshape(groups, heads_here, 2 * GROUP, DK)
    )
    value_blk = (
        reflection_value_rows.reshape(2, groups, GROUP, heads_here, DV)
        .transpose(1, 3, 2, 0, 4)
        .reshape(groups, heads_here, 2 * GROUP, DV)
    )
    gate_strength_slab = (
        (2.0 * jax.nn.sigmoid(beta_logit))
        .reshape(2, heads_here, groups, GROUP)
        .transpose(2, 1, 3, 0)
        .reshape(groups, heads_here, 2 * GROUP)
    )
    transition, pushed, query_eff, inner_portion = group_terms(
        query_blk, key_blk, value_blk, gate_strength_slab
    )
    identity_mat = jnp.broadcast_to(jnp.eye(DK, dtype=jnp.float32), (heads_here, DK, DK))
    empty_state = jnp.zeros((heads_here, DK, DV), jnp.float32)

    def compose(pair_acc, group_pair):
        acc_trans, acc_state = pair_acc
        step_trans, step_push = group_pair
        return (
            (matmul_hi(step_trans, acc_trans), matmul_hi(step_trans, acc_state) + step_push),
            pair_acc,
        )

    (device_trans, device_state), (prior_trans, prior_state) = lax.scan(
        compose, (identity_mat, empty_state), (transition, pushed)
    )

    def relay_state(count_now, arriving):
        leaving = matmul_hi(device_trans, arriving) + device_state
        return from_behind(leaving, "ctx", 1)

    incoming = lax.fori_loop(0, lax.axis_size("ctx") - 1, relay_state, empty_state)

    def replay(memory, group_in):
        step_trans, step_push, step_query, step_inner = group_in
        return (
            matmul_hi(step_trans, memory) + step_push,
            matmul_hi(step_query, memory) + step_inner,
        )

    _, outputs = lax.scan(replay, incoming, (transition, pushed, query_eff, inner_portion))
    head_out = outputs.transpose(0, 2, 1, 3).reshape(tok_local, heads_here * DV)
    square_sum = jnp.sum(head_out * head_out, axis=-1)
    total_square = lax.psum(square_sum, "head")
    return head_out * lax.rsqrt(total_square / (HEADS * DV) + 1e-05)[:, None]


def solution(mesh):
    placed = (
        P("ctx", "head"),
        P(None, "ctx", "head"),
        P(None, "ctx", "head"),
        P(None, "head", "ctx"),
    )
    return jax.shard_map(
        local, mesh=mesh, in_specs=placed, out_specs=P("ctx", "head"), check_vma=False
    )
```

profile of v0, /device:TPU:31, one launch (start us, length us, event | category | flops | bytes accessed | tf_op | source)
XLA Modules:
  0.0 1146.6 jit_solution(11722219085245825025)
XLA Ops:
  0.0 3.1 copy.48
  5.7 5.2 copy.33
  11.3 14.5 %add_bitcast_fusion = f32[4,16,1,128,128]{4,3,2,1,0:T(8,128)} fusion(f32[4,16,128,128]{3,2,1,0:T(8,128)} %bitcast.109, f32[128,128]{1,0:T(8,128)S(1)} %get-tuple-element.149, f32[4,16,128]{2,1,0:T(8,128)S(1)} %copy.35, f32[128,128]{1,0:T(8,128)S(1)} %get-tuple-element.148, pred[128,128]{1,0:T(8,128)(4,1)S(1)} %get-tuple-element.146, ...), kind=kOutput, calls=%fused_computation.29 | convolution fusion | flops 1615855616 | bytes 8585216 | tf_op jit(solution)/shard_map/...id,...jd->...ij/dot_general | solution.py:34
  25.7 630.7 %custom-call.4 = f32[4,16,1,128,128]{3,4,2,1,0:T(8,128)} custom-call(f32[4,16,1,128,128]{4,3,2,1,0:T(8,128)} %add_bitcast_fusion), custom_call_target="InvertDiagBlocksLowerTriangular" | custom-call | tf_op jit(solution)/shard_map/jit(_solve_triangular)/vmap(vmap())/triangular_solve | solution.py:42
  656.4 3.1 copy.49
  659.5 5.2 copy.37
  664.7 11.0 fusion.19
  675.7 8.7 fusion.32
  684.4 8.3 fusion.26
  692.8 21.1 %while.40 = (s32[]{:T(128)}, f32[16,128,128]{2,1,0:T(8,128)S(1)}, f32[16,128,128]{2,1,0:T(8,128)S(1)}, f32[4,16,128,128]{3,2,1,0:T(8,128)}, f32[4,16,128,128]{3,2,1,0:T(8,128)}) while((s32[]{:T(128)}, f32[16,128,128]{2,1,0:T(8,128)S(1)}, f32[16,128,128]{2,1,0:T(8,128)S(1)}, f32[4,16,128,128]{3,2,1,0:T(8,128)}, ...), condition=%wide.region_2.3_spmd.clone.clone, body=%wide.region_1.0_spmd.clone.sunk.clone | while | flops 805830656 | bytes 11535943 | solution.py:96
  692.9 2.7 convolution_add_fusion.12
  695.7 2.4 fusion.98
  698.2 2.7 convolution_add_fusion.12
  701.0 2.4 fusion.98
  703.4 2.7 convolution_add_fusion.12
  706.2 2.4 fusion.98
  708.7 2.7 convolution_add_fusion.12
  711.5 2.4 fusion.98
  714.0 363.0 %while.38 = (s32[]{:T(128)}, f32[16,128,128]{2,1,0:T(8,128)S(1)}, f32[16,128,128]{2,1,0:T(8,128)S(1)}, f32[16,128,128]{2,1,0:T(8,128)S(1)}) while((s32[]{:T(128)}, f32[16,128,128]{2,1,0:T(8,128)S(1)}, f32[16,128,128]{2,1,0:T(8,128)S(1)}, f32[16,128,128]{2,1,0:T(8,128)S(1)}) %tuple.63), condition=%wide.region_4.5_spmd.clone, body=%wide.region_3.4_spmd.sunk.clone | while | flops 402915328 | bytes 8388701 | solution.py:104
  714.0 2.1 convolution_add_fusion.10
  717.4 24.8 %collective-permute-done = f32[16,128,128]{2,1,0:T(8,128)S(1)} collective-permute-done((f32[16,128,128]{2,1,0:T(8,128)}, f32[16,128,128]{2,1,0:T(8,128)S(1)}, u32[]{:S(2)}, u32[]{:S(2)}) %collective-permute-start) | collective-permute-done | bytes 1048608 | tf_op jit(solution)/shard_map/while/body/eval_jaxpr/ppermute | solution.py:18
  742.3 2.1 convolution_add_fusion.10
  745.7 23.9 %collective-permute-done = f32[16,128,128]{2,1,0:T(8,128)S(1)} collective-permute-done((f32[16,128,128]{2,1,0:T(8,128)}, f32[16,128,128]{2,1,0:T(8,128)S(1)}, u32[]{:S(2)}, u32[]{:S(2)}) %collective-permute-start) | collective-permute-done | bytes 1048608 | tf_op jit(solution)/shard_map/while/body/eval_jaxpr/ppermute | solution.py:18
  769.6 2.1 convolution_add_fusion.10
  773.0 23.9 %collective-permute-done = f32[16,128,128]{2,1,0:T(8,128)S(1)} collective-permute-done((f32[16,128,128]{2,1,0:T(8,128)}, f32[16,128,128]{2,1,0:T(8,128)S(1)}, u32[]{:S(2)}, u32[]{:S(2)}) %collective-permute-start) | collective-permute-done | bytes 1048608 | tf_op jit(solution)/shard_map/while/body/eval_jaxpr/ppermute | solution.py:18
  796.9 2.1 convolution_add_fusion.10
  800.3 23.0 %collective-permute-done = f32[16,128,128]{2,1,0:T(8,128)S(1)} collective-permute-done((f32[16,128,128]{2,1,0:T(8,128)}, f32[16,128,128]{2,1,0:T(8,128)S(1)}, u32[]{:S(2)}, u32[]{:S(2)}) %collective-permute-start) | collective-permute-done | bytes 1048608 | tf_op jit(solution)/shard_map/while/body/eval_jaxpr/ppermute | solution.py:18
  823.2 2.1 convolution_add_fusion.10
  826.7 22.0 %collective-permute-done = f32[16,128,128]{2,1,0:T(8,128)S(1)} collective-permute-done((f32[16,128,128]{2,1,0:T(8,128)}, f32[16,128,128]{2,1,0:T(8,128)S(1)}, u32[]{:S(2)}, u32[]{:S(2)}) %collective-permute-start) | collective-permute-done | bytes 1048608 | tf_op jit(solution)/shard_map/while/body/eval_jaxpr/ppermute | solution.py:18
  848.7 2.1 convolution_add_fusion.10
  852.1 21.1 %collective-permute-done = f32[16,128,128]{2,1,0:T(8,128)S(1)} collective-permute-done((f32[16,128,128]{2,1,0:T(8,128)}, f32[16,128,128]{2,1,0:T(8,128)S(1)}, u32[]{:S(2)}, u32[]{:S(2)}) %collective-permute-start) | collective-permute-done | bytes 1048608 | tf_op jit(solution)/shard_map/while/body/eval_jaxpr/ppermute | solution.py:18
  873.2 2.1 convolution_add_fusion.10
  876.7 21.9 %collective-permute-done = f32[16,128,128]{2,1,0:T(8,128)S(1)} collective-permute-done((f32[16,128,128]{2,1,0:T(8,128)}, f32[16,128,128]{2,1,0:T(8,128)S(1)}, u32[]{:S(2)}, u32[]{:S(2)}) %collective-permute-start) | collective-permute-done | bytes 1048608 | tf_op jit(solution)/shard_map/while/body/eval_jaxpr/ppermute | solution.py:18
  898.5 2.1 convolution_add_fusion.10
  902.0 20.2 %collective-permute-done = f32[16,128,128]{2,1,0:T(8,128)S(1)} collective-permute-done((f32[16,128,128]{2,1,0:T(8,128)}, f32[16,128,128]{2,1,0:T(8,128)S(1)}, u32[]{:S(2)}, u32[]{:S(2)}) %collective-permute-start) | collective-permute-done | bytes 1048608 | tf_op jit(solution)/shard_map/while/body/eval_jaxpr/ppermute | solution.py:18
  922.1 2.1 convolution_add_fusion.10
  925.5 19.3 %collective-permute-done = f32[16,128,128]{2,1,0:T(8,128)S(1)} collective-permute-done((f32[16,128,128]{2,1,0:T(8,128)}, f32[16,128,128]{2,1,0:T(8,128)S(1)}, u32[]{:S(2)}, u32[]{:S(2)}) %collective-permute-start) | collective-permute-done | bytes 1048608 | tf_op jit(solution)/shard_map/while/body/eval_jaxpr/ppermute | solution.py:18
  944.8 2.1 convolution_add_fusion.10
  948.2 18.3 %collective-permute-done = f32[16,128,128]{2,1,0:T(8,128)S(1)} collective-permute-done((f32[16,128,128]{2,1,0:T(8,128)}, f32[16,128,128]{2,1,0:T(8,128)S(1)}, u32[]{:S(2)}, u32[]{:S(2)}) %collective-permute-start) | collective-permute-done | bytes 1048608 | tf_op jit(solution)/shard_map/while/body/eval_jaxpr/ppermute | solution.py:18
  966.5 2.1 convolution_add_fusion.10
  969.9 18.2 %collective-permute-done = f32[16,128,128]{2,1,0:T(8,128)S(1)} collective-permute-done((f32[16,128,128]{2,1,0:T(8,128)}, f32[16,128,128]{2,1,0:T(8,128)S(1)}, u32[]{:S(2)}, u32[]{:S(2)}) %collective-permute-start) | collective-permute-done | bytes 1048608 | tf_op jit(solution)/shard_map/while/body/eval_jaxpr/ppermute | solution.py:18
  988.2 2.1 convolution_add_fusion.10
  991.6 18.2 %collective-permute-done = f32[16,128,128]{2,1,0:T(8,128)S(1)} collective-permute-done((f32[16,128,128]{2,1,0:T(8,128)}, f32[16,128,128]{2,1,0:T(8,128)S(1)}, u32[]{:S(2)}, u32[]{:S(2)}) %collective-permute-start) | collective-permute-done | bytes 1048608 | tf_op jit(solution)/shard_map/while/body/eval_jaxpr/ppermute | solution.py:18
  1009.8 2.1 convolution_add_fusion.10
  1013.2 18.2 %collective-permute-done = f32[16,128,128]{2,1,0:T(8,128)S(1)} collective-permute-done((f32[16,128,128]{2,1,0:T(8,128)}, f32[16,128,128]{2,1,0:T(8,128)S(1)}, u32[]{:S(2)}, u32[]{:S(2)}) %collective-permute-start) | collective-permute-done | bytes 1048608 | tf_op jit(solution)/shard_map/while/body/eval_jaxpr/ppermute | solution.py:18
  1031.4 2.1 convolution_add_fusion.10
  1034.8 18.7 %collective-permute-done = f32[16,128,128]{2,1,0:T(8,128)S(1)} collective-permute-done((f32[16,128,128]{2,1,0:T(8,128)}, f32[16,128,128]{2,1,0:T(8,128)S(1)}, u32[]{:S(2)}, u32[]{:S(2)}) %collective-permute-start) | collective-permute-done | bytes 1048608 | tf_op jit(solution)/shard_map/while/body/eval_jaxpr/ppermute | solution.py:18
  1053.5 2.1 convolution_add_fusion.10
  1056.9 19.9 %collective-permute-done = f32[16,128,128]{2,1,0:T(8,128)S(1)} collective-permute-done((f32[16,128,128]{2,1,0:T(8,128)}, f32[16,128,128]{2,1,0:T(8,128)S(1)}, u32[]{:S(2)}, u32[]{:S(2)}) %collective-permute-start) | collective-permute-done | bytes 1048608 | tf_op jit(solution)/shard_map/while/body/eval_jaxpr/ppermute | solution.py:18
  1079.7 10.1 fusion.35
  1089.9 7.1 bitcast_subtract_fusion
  1096.9 4.1 fusion.24
  1101.0 23.4 %while.39 = (s32[]{:T(128)}, f32[16,128,128]{2,1,0:T(8,128)S(1)}, f32[4,16,64,128]{3,2,1,0:T(8,128)}, f32[4,16,128,128]{3,2,1,0:T(8,128)}, f32[4,16,128,128]{3,2...) while((s32[]{:T(128)}, f32[16,128,128]{2,1,0:T(8,128)S(1)}, ...), condition=%wide.region_7.8_spmd.clone, body=%wide.region_6.7_spmd.sunk.clone | while | flops 604372992 | bytes 8915021 | solution.py:113
  1101.4 3.0 fusion.93
  1104.3 2.7 convolution_add_fusion.11
  1107.2 3.0 fusion.93
  1110.1 2.7 convolution_add_fusion.11
  1113.0 3.0 fusion.93
  1115.9 2.7 convolution_add_fusion.11
  1118.8 3.0 fusion.93
  1121.7 2.7 convolution_add_fusion.11
  1124.5 3.0 copy.43
  1127.8 16.1 %psum.7 = f32[256]{0:T(256)S(1)} all-reduce(f32[256]{0:T(256)S(1)} %reduce_sum.32), channel_id=1, replica_groups=mesh['ctx'=16,'head'=2] {'head'}, use_global_device_ids=true, to_apply=%region_9.10 | all-reduce | flops 256 | bytes 2048 | tf_op jit(solution)/shard_map/psum | solution.py:116
  1143.9 2.3 bitcast_multiply_fusion
  (63 shorter events, 26.3 us)
Async XLA Ops:
  5.7 5.2 copy-start.3
  659.5 5.2 copy-start
  675.7 8.7 copy-start.1
  716.2 26.1 %collective-permute-start = (f32[16,128,128]{2,1,0:T(8,128)}, f32[16,128,128]{2,1,0:T(8,128)S(1)}, u32[]{:S(2)}, u32[]{:S(2)}) collective-permute-start(f32[16,128,128]{2,1,0:T(8,128)} %convolution_add_fusion.10), channel_id=1, source_target_pairs={{0,2},{2,4},{4,6},{6,8},{8,10},{10,12},{12,14},{14,16},{16,18},{18... | collective-permute-start | bytes 3145736 | tf_op jit(solution)/shard_map/while/body/eval_jaxpr/ppermute | solution.py:18
  744.4 25.2 %collective-permute-start = (f32[16,128,128]{2,1,0:T(8,128)}, f32[16,128,128]{2,1,0:T(8,128)S(1)}, u32[]{:S(2)}, u32[]{:S(2)}) collective-permute-start(f32[16,128,128]{2,1,0:T(8,128)} %convolution_add_fusion.10), channel_id=1, source_target_pairs={{0,2},{2,4},{4,6},{6,8},{8,10},{10,12},{12,14},{14,16},{16,18},{18... | collective-permute-start | bytes 3145736 | tf_op jit(solution)/shard_map/while/body/eval_jaxpr/ppermute | solution.py:18
  771.7 25.2 %collective-permute-start = (f32[16,128,128]{2,1,0:T(8,128)}, f32[16,128,128]{2,1,0:T(8,128)S(1)}, u32[]{:S(2)}, u32[]{:S(2)}) collective-permute-start(f32[16,128,128]{2,1,0:T(8,128)} %convolution_add_fusion.10), channel_id=1, source_target_pairs={{0,2},{2,4},{4,6},{6,8},{8,10},{10,12},{12,14},{14,16},{16,18},{18... | collective-permute-start | bytes 3145736 | tf_op jit(solution)/shard_map/while/body/eval_jaxpr/ppermute | solution.py:18
  799.0 24.3 %collective-permute-start = (f32[16,128,128]{2,1,0:T(8,128)}, f32[16,128,128]{2,1,0:T(8,128)S(1)}, u32[]{:S(2)}, u32[]{:S(2)}) collective-permute-start(f32[16,128,128]{2,1,0:T(8,128)} %convolution_add_fusion.10), channel_id=1, source_target_pairs={{0,2},{2,4},{4,6},{6,8},{8,10},{10,12},{12,14},{14,16},{16,18},{18... | collective-permute-start | bytes 3145736 | tf_op jit(solution)/shard_map/while/body/eval_jaxpr/ppermute | solution.py:18
  825.4 23.3 %collective-permute-start = (f32[16,128,128]{2,1,0:T(8,128)}, f32[16,128,128]{2,1,0:T(8,128)S(1)}, u32[]{:S(2)}, u32[]{:S(2)}) collective-permute-start(f32[16,128,128]{2,1,0:T(8,128)} %convolution_add_fusion.10), channel_id=1, source_target_pairs={{0,2},{2,4},{4,6},{6,8},{8,10},{10,12},{12,14},{14,16},{16,18},{18... | collective-permute-start | bytes 3145736 | tf_op jit(solution)/shard_map/while/body/eval_jaxpr/ppermute | solution.py:18
  850.8 22.4 %collective-permute-start = (f32[16,128,128]{2,1,0:T(8,128)}, f32[16,128,128]{2,1,0:T(8,128)S(1)}, u32[]{:S(2)}, u32[]{:S(2)}) collective-permute-start(f32[16,128,128]{2,1,0:T(8,128)} %convolution_add_fusion.10), channel_id=1, source_target_pairs={{0,2},{2,4},{4,6},{6,8},{8,10},{10,12},{12,14},{14,16},{16,18},{18... | collective-permute-start | bytes 3145736 | tf_op jit(solution)/shard_map/while/body/eval_jaxpr/ppermute | solution.py:18
  875.4 23.2 %collective-permute-start = (f32[16,128,128]{2,1,0:T(8,128)}, f32[16,128,128]{2,1,0:T(8,128)S(1)}, u32[]{:S(2)}, u32[]{:S(2)}) collective-permute-start(f32[16,128,128]{2,1,0:T(8,128)} %convolution_add_fusion.10), channel_id=1, source_target_pairs={{0,2},{2,4},{4,6},{6,8},{8,10},{10,12},{12,14},{14,16},{16,18},{18... | collective-permute-start | bytes 3145736 | tf_op jit(solution)/shard_map/while/body/eval_jaxpr/ppermute | solution.py:18
  900.7 21.4 %collective-permute-start = (f32[16,128,128]{2,1,0:T(8,128)}, f32[16,128,128]{2,1,0:T(8,128)S(1)}, u32[]{:S(2)}, u32[]{:S(2)}) collective-permute-start(f32[16,128,128]{2,1,0:T(8,128)} %convolution_add_fusion.10), channel_id=1, source_target_pairs={{0,2},{2,4},{4,6},{6,8},{8,10},{10,12},{12,14},{14,16},{16,18},{18... | collective-permute-start | bytes 3145736 | tf_op jit(solution)/shard_map/while/body/eval_jaxpr/ppermute | solution.py:18
  924.2 20.5 %collective-permute-start = (f32[16,128,128]{2,1,0:T(8,128)}, f32[16,128,128]{2,1,0:T(8,128)S(1)}, u32[]{:S(2)}, u32[]{:S(2)}) collective-permute-start(f32[16,128,128]{2,1,0:T(8,128)} %convolution_add_fusion.10), channel_id=1, source_target_pairs={{0,2},{2,4},{4,6},{6,8},{8,10},{10,12},{12,14},{14,16},{16,18},{18... | collective-permute-start | bytes 3145736 | tf_op jit(solution)/shard_map/while/body/eval_jaxpr/ppermute | solution.py:18
  946.9 19.6 %collective-permute-start = (f32[16,128,128]{2,1,0:T(8,128)}, f32[16,128,128]{2,1,0:T(8,128)S(1)}, u32[]{:S(2)}, u32[]{:S(2)}) collective-permute-start(f32[16,128,128]{2,1,0:T(8,128)} %convolution_add_fusion.10), channel_id=1, source_target_pairs={{0,2},{2,4},{4,6},{6,8},{8,10},{10,12},{12,14},{14,16},{16,18},{18... | collective-permute-start | bytes 3145736 | tf_op jit(solution)/shard_map/while/body/eval_jaxpr/ppermute | solution.py:18
  968.7 19.5 %collective-permute-start = (f32[16,128,128]{2,1,0:T(8,128)}, f32[16,128,128]{2,1,0:T(8,128)S(1)}, u32[]{:S(2)}, u32[]{:S(2)}) collective-permute-start(f32[16,128,128]{2,1,0:T(8,128)} %convolution_add_fusion.10), channel_id=1, source_target_pairs={{0,2},{2,4},{4,6},{6,8},{8,10},{10,12},{12,14},{14,16},{16,18},{18... | collective-permute-start | bytes 3145736 | tf_op jit(solution)/shard_map/while/body/eval_jaxpr/ppermute | solution.py:18
  990.3 19.5 %collective-permute-start = (f32[16,128,128]{2,1,0:T(8,128)}, f32[16,128,128]{2,1,0:T(8,128)S(1)}, u32[]{:S(2)}, u32[]{:S(2)}) collective-permute-start(f32[16,128,128]{2,1,0:T(8,128)} %convolution_add_fusion.10), channel_id=1, source_target_pairs={{0,2},{2,4},{4,6},{6,8},{8,10},{10,12},{12,14},{14,16},{16,18},{18... | collective-permute-start | bytes 3145736 | tf_op jit(solution)/shard_map/while/body/eval_jaxpr/ppermute | solution.py:18
  1011.9 19.5 %collective-permute-start = (f32[16,128,128]{2,1,0:T(8,128)}, f32[16,128,128]{2,1,0:T(8,128)S(1)}, u32[]{:S(2)}, u32[]{:S(2)}) collective-permute-start(f32[16,128,128]{2,1,0:T(8,128)} %convolution_add_fusion.10), channel_id=1, source_target_pairs={{0,2},{2,4},{4,6},{6,8},{8,10},{10,12},{12,14},{14,16},{16,18},{18... | collective-permute-start | bytes 3145736 | tf_op jit(solution)/shard_map/while/body/eval_jaxpr/ppermute | solution.py:18
  1033.5 20.0 %collective-permute-start = (f32[16,128,128]{2,1,0:T(8,128)}, f32[16,128,128]{2,1,0:T(8,128)S(1)}, u32[]{:S(2)}, u32[]{:S(2)}) collective-permute-start(f32[16,128,128]{2,1,0:T(8,128)} %convolution_add_fusion.10), channel_id=1, source_target_pairs={{0,2},{2,4},{4,6},{6,8},{8,10},{10,12},{12,14},{14,16},{16,18},{18... | collective-permute-start | bytes 3145736 | tf_op jit(solution)/shard_map/while/body/eval_jaxpr/ppermute | solution.py:18
  1055.6 21.2 %collective-permute-start = (f32[16,128,128]{2,1,0:T(8,128)}, f32[16,128,128]{2,1,0:T(8,128)S(1)}, u32[]{:S(2)}, u32[]{:S(2)}) collective-permute-start(f32[16,128,128]{2,1,0:T(8,128)} %convolution_add_fusion.10), channel_id=1, source_target_pairs={{0,2},{2,4},{4,6},{6,8},{8,10},{10,12},{12,14},{14,16},{16,18},{18... | collective-permute-start | bytes 3145736 | tf_op jit(solution)/shard_map/while/body/eval_jaxpr/ppermute | solution.py:18
  1079.7 17.2 %slice-start = ((s8[8388608]{0:T(1024)(128)(4,1)}), s8[4194304]{0:T(1024)(128)(4,1)S(1)}, s32[]{:S(2)}) async-start(s8[8388608]{0:T(1024)(128)(4,1)} %bitcast.114), calls=%async_computation | async-start | bytes 8388608
  1089.8 7.1 slice-start.1
  1124.5 3.0 copy-start.2
where the time goes:
time: 1170 us; the launch traced here: 1150 us
  other arithmetic  637 us (54%)
  waiting for transfers between devices  312 us (27%)
  matrix products  139 us (12%)
  local copies, waits for them, and re-layouts  23.1 us (2%)
  starting transfers between devices  19.2 us (2%)
  blocking collectives  16.1 us (1%)
    another operation x2, other arithmetic, group_terms(): jax.scipy.linalg.solve_triangular(unit_lower, right_cols, lower=True, uni...  631 us
    ppermute x15, waiting for transfers between devices, from_behind(): lax.ppermute(value, axis, [(source, source + steps) for source in range(i...  312 us
    dot_general x33, matrix products, matmul_hi(): return jnp.einsum('...ij,...jk->...ik', left, right, precision=highest_mode)  86.1 us
  transfers between devices with their start and end apart: 15, of which 15 were waited for; matrix products, arithmetic and copies ran while one was open for 0% of the time, Pallas kernels for 0%

commit v1 on v0

v1 whole, which is shorter than its diff:
```python
import functools

import jax
import jax.numpy as jnp
from jax import lax
from jax.experimental import pallas as pl
from jax.experimental.pallas import tpu as pltpu
from jax.sharding import PartitionSpec as P

DK = 128
DV = 128
GROUP = 64
SUB = 2 * GROUP
F32 = jnp.float32
BF16 = jnp.bfloat16
MESH = pl.DeviceIdType.MESH
VMEM_LIMIT = 48 * 1024 * 1024


def split(x):
    high = x.astype(BF16)
    return high, (x - high.astype(F32)).astype(BF16)


def wide(x):
    return jnp.concatenate(split(x), axis=1)


def tall(x):
    row = jnp.concatenate(split(x), axis=1)
    return jnp.concatenate([row, row], axis=0)


def product(left, right):
    both = jnp.dot(left, right, preferred_element_type=F32)
    width = both.shape[1] // 2
    return both[:, :width] + both[:, width:]


def terms_kernel(q_ref, k_ref, v_ref, b_ref, trans_ref, state_ref, qeff_ref, inner_ref):
    tokens = q_ref.shape[0]
    groups = range(tokens // GROUP)
    row = lax.broadcasted_iota(jnp.int32, (SUB, SUB), 0)
    col = lax.broadcasted_iota(jnp.int32, (SUB, SUB), 1)
    row_order = 2 * (row % GROUP) + row // GROUP
    col_order = 2 * (col % GROUP) + col // GROUP
    strict = row_order > col_order
    differ = row_order ^ col_order
    eye = jnp.where(row == col, 1.0, 0.0).astype(F32)
    token = lax.broadcasted_iota(jnp.int32, (GROUP, SUB), 0)
    key_token = lax.broadcasted_iota(jnp.int32, (GROUP, SUB), 1) % GROUP
    visible = key_token <= token

    query, key_t, right, lower, masked, inverse = [], [], [], [], [], []
    for g in groups:
        rows = slice(g * GROUP, (g + 1) * GROUP)
        q = q_ref[rows, :]
        q = q * lax.rsqrt(jnp.sum(q * q, axis=-1, keepdims=True) + 1e-06)
        k = jnp.concatenate([k_ref[0, rows, :], k_ref[1, rows, :]], axis=0)
        k = k * lax.rsqrt(jnp.sum(k * k, axis=-1, keepdims=True) + 1e-06)
        v = jnp.concatenate([v_ref[0, rows, :], v_ref[1, rows, :]], axis=0)
        beta = jnp.concatenate([b_ref[0, rows, 0:1], b_ref[0, rows, 1:2]], axis=0)
        kb = k * beta
        kt = k.T
        both = product(wide(jnp.concatenate([kb, q], axis=0)), tall(kt))
        low = jnp.where(strict, both[:SUB], 0.0)
        query.append(q)
        key_t.append(kt)
        right.append(jnp.concatenate([v * beta, kb], axis=1))
        lower.append(low)
        masked.append(jnp.where(visible, both[SUB:], 0.0))
        inverse.append(eye - jnp.where(differ == 1, low, 0.0))

    level = 1
    while (1 << level) < SUB:
        pick = (differ >> level) == 1
        step = [
            product(wide(jnp.where(pick, lower[g], 0.0)), tall(inverse[g])) for g in groups
        ]
        inverse = [
            inverse[g] - product(wide(inverse[g]), tall(step[g])) for g in groups
        ]
        level += 1

    solved = [product(wide(inverse[g]), tall(right[g])) for g in groups]
    terms = [
        product(wide(jnp.concatenate([key_t[g], masked[g]], axis=0)), tall(solved[g]))
        for g in groups
    ]
    prefix = None
    for g in groups:
        rows = slice(g * GROUP, (g + 1) * GROUP)
        pushed, inner = terms[g][:SUB, :DV], terms[g][SUB:, :DV]
        trans, qeff = eye - terms[g][:SUB, DV:], query[g] - terms[g][SUB:, DV:]
        if prefix is not None:
            moved = product(wide(jnp.concatenate([trans, qeff], axis=0)), tall(prefix))
            pushed = pushed + moved[:SUB, DK:]
            inner = inner + moved[SUB:, DK:]
            trans, qeff = moved[:SUB, :DK], moved[SUB:, :DK]
        qeff_ref[0, rows, :] = wide(qeff)
        inner_ref[rows, :] = inner
        prefix = jnp.concatenate([trans, pushed], axis=1)
    trans_ref[0] = wide(trans)
    state_ref[0] = pushed


def chain_kernel(
    ctx_n, head_n, width, trans_ref, state_ref, qeff_ref, inner_ref, out_ref,
    arriving, leaving, mine, theirs, send_sem, recv_sem, sum_send, sum_recv,
):
    heads, tokens = qeff_ref.shape[:2]
    me = lax.axis_index("ctx")
    core = lax.axis_index("head")
    peers = [lax.rem(core + off, head_n) for off in range(1, head_n)]

    barrier = pltpu.get_barrier_semaphore()
    for peer in peers:
        pl.semaphore_signal(barrier, inc=1, device_id=(me, peer), device_id_type=MESH)

    @pl.when(me > 0)
    def _():
        pl.semaphore_signal(barrier, inc=1, device_id=(me - 1, core), device_id_type=MESH)

    @pl.when(me < ctx_n - 1)
    def _():
        pl.semaphore_signal(barrier, inc=1, device_id=(me + 1, core), device_id_type=MESH)

    @pl.when(me == 0)
    def _():
        arriving[...] = jnp.zeros_like(arriving)

    neighbours = jnp.minimum(me, 1) + jnp.minimum(ctx_n - 1 - me, 1)
    pl.semaphore_wait(barrier, neighbours + (head_n - 1))

    mine[...] = jnp.zeros_like(mine)

    def copy_of(h, target):
        return pltpu.make_async_remote_copy(
            src_ref=leaving.at[h],
            dst_ref=arriving.at[h],
            send_sem=send_sem.at[h],
            recv_sem=recv_sem.at[h],
            device_id=(target, core),
            device_id_type=MESH,
        )

    def one_head(h, carry):
        @pl.when(me > 0)
        def _():
            copy_of(h, me).wait_recv()

        state = tall(arriving[h])

        @pl.when(me < ctx_n - 1)
        def _():
            leaving[h] = product(trans_ref[h], state) + state_ref[h]
            copy_of(h, me + 1).start()

        columns = pl.ds(pl.multiple_of(h * DV, DV), DV)
        read = product(qeff_ref[h], state) + inner_ref[:, columns]
        out_ref[:, columns] = read
        mine[...] += read * read
        return carry

    lax.fori_loop(0, heads, one_head, 0)

    def sum_copy(off):
        return pltpu.make_async_remote_copy(
            src_ref=mine,
            dst_ref=theirs.at[off],
            send_sem=sum_send.at[off],
            recv_sem=sum_recv.at[off],
            device_id=(me, peers[off]),
            device_id_type=MESH,
        )

    for off in range(head_n - 1):
        sum_copy(off).start()
    for off in range(head_n - 1):
        sum_copy(off).wait()

    total = mine[...]
    for off in range(head_n - 1):
        total = total + theirs[off]
    scale = lax.rsqrt(jnp.sum(total, axis=-1, keepdims=True) / width + 1e-05)
    scale = jnp.broadcast_to(scale, (tokens, DV))

    def scale_head(h, carry):
        columns = pl.ds(pl.multiple_of(h * DV, DV), DV)
        out_ref[:, columns] = out_ref[:, columns] * scale
        return carry

    lax.fori_loop(0, heads, scale_head, 0)

    @pl.when(me < ctx_n - 1)
    def _():
        def finish(h, carry):
            copy_of(h, me + 1).wait_send()
            return carry

        lax.fori_loop(0, heads, finish, 0)


def local(query_rows, key_rows, reflection_value_rows, beta_logit):
    tokens = query_rows.shape[0]
    heads = query_rows.shape[1] // DK
    ctx_n = lax.axis_size("ctx")
    head_n = lax.axis_size("head")
    beta = (2.0 * jax.nn.sigmoid(beta_logit)).transpose(1, 2, 0)
    shape = jax.ShapeDtypeStruct
    rows_of = pl.BlockSpec((tokens, DK), lambda h: (0, h))
    pair_of = pl.BlockSpec((2, tokens, DK), lambda h: (0, 0, h))

    def head_of(*block):
        return pl.BlockSpec((1,) + block, lambda h: (h, 0, 0))

    trans, state, qeff, inner = pl.pallas_call(
        terms_kernel,
        grid=(heads,),
        in_specs=[rows_of, pair_of, pair_of, head_of(tokens, 2)],
        out_specs=[head_of(DK, 2 * DK), head_of(DK, DV), head_of(tokens, 2 * DK), rows_of],
        out_shape=[
            shape((heads, DK, 2 * DK), BF16),
            shape((heads, DK, DV), F32),
            shape((heads, tokens, 2 * DK), BF16),
            shape((tokens, heads * DV), F32),
        ],
        compiler_params=pltpu.CompilerParams(vmem_limit_bytes=VMEM_LIMIT),
        name="terms",
    )(query_rows, key_rows, reflection_value_rows, beta)

    whole = pl.BlockSpec(memory_space=pltpu.VMEM)
    width = float(head_n * heads * DV)
    return pl.pallas_call(
        functools.partial(chain_kernel, ctx_n, head_n, width),
        in_specs=[whole] * 4,
        out_specs=whole,
        out_shape=shape((tokens, heads * DV), F32),
        scratch_shapes=[
            pltpu.VMEM((heads, DK, DV), F32),
            pltpu.VMEM((heads, DK, DV), F32),
            pltpu.VMEM((tokens, DV), F32),
            pltpu.VMEM((max(head_n - 1, 1), tokens, DV), F32),
            pltpu.SemaphoreType.DMA((heads,)),
            pltpu.SemaphoreType.DMA((heads,)),
            pltpu.SemaphoreType.DMA((max(head_n - 1, 1),)),
            pltpu.SemaphoreType.DMA((max(head_n - 1, 1),)),
        ],
        compiler_params=pltpu.CompilerParams(
            collective_id=0, has_side_effects=True, vmem_limit_bytes=VMEM_LIMIT
        ),
        name="chain",
    )(trans, state, qeff, inner)


def solution(mesh):
    placed = (
        P("ctx", "head"),
        P(None, "ctx", "head"),
        P(None, "ctx", "head"),
        P(None, "head", "ctx"),
    )
    return jax.shard_map(
        local, mesh=mesh, in_specs=placed, out_specs=P("ctx", "head"), check_vma=False
    )
```

time: 1170 us -> 151 us (0.13); the launches traced: 1150 us -> 150 us
  other arithmetic: 637 us -> 1.88 us
  waiting for transfers between devices: 312 us -> 0 us
  Pallas kernels: 0 us -> 144 us
  matrix products: 139 us -> 0 us
  starting transfers between devices: 19.2 us -> 0 us
  local copies, waits for them, and re-layouts: 23.1 us -> 4.02 us
  blocking collectives: 16.1 us -> 0 us
    another operation x2 -> x0, other arithmetic: 631 us -> none  [group_terms(): jax.scipy.linalg.solve_triangular(unit_lower, right_cols, lower=True, uni...]
    ppermute x15 -> x0, waiting for transfers between devices: 312 us -> none  [from_behind(): lax.ppermute(value, axis, [(source, source + steps) for source in range(i...]
    pallas_call x0 -> x2, Pallas kernels: none -> 144 us  [the longest x1 82.4 us: local(): pl.pallas_call(functools.partial(chain_kernel, ctx_n, head_n, width), in_...]
    dot_general x37 -> x0, matrix products: 128 us -> none  [the longest x33 86.1 us: matmul_hi(): return jnp.einsum('...ij,...jk->...ik', left, right, precision=highest_mode)]
    ppermute x15 -> x0, starting transfers between devices: 19.2 us -> none  [from_behind(): lax.ppermute(value, axis, [(source, source + steps) for source in range(i...]
    psum x1 -> x0, blocking collectives: 16.1 us -> none  [local(): total_square = lax.psum(square_sum, 'head')]
    transpose x3 -> x0, local copies, waits for them, and re-layouts: 13.3 us -> none  [the longest x1 5.2 us: local(): value_blk = reflection_value_rows.reshape(2, groups, GROUP, heads_here, D...]
  transfers between devices with their start and end apart: 15 -> 0, of which waited for: 15 -> 0; matrix products, arithmetic and copies ran while one was open for 0% -> 0% of each run, Pallas kernels for 0% -> 0%
where the time goes in v1:
time: 151 us; the launch traced here: 150 us
  Pallas kernels  144 us (95%)
  local copies, waits for them, and re-layouts  4.02 us (3%)
  other arithmetic  1.88 us (1%)
    pallas_call x1, Pallas kernels, local(): pl.pallas_call(functools.partial(chain_kernel, ctx_n, head_n, width), in_...  82.4 us
    pallas_call x1, Pallas kernels, local(): pl.pallas_call(terms_kernel, grid=(heads,), in_specs=[rows_of, pair_of, p...  62.1 us
    unnamed x4, local copies, waits for them, and re-layouts  4.02 us

profile of v1, /device:TPU:31, one launch (start us, length us, event | category | flops | bytes accessed | tf_op | source)
XLA Modules:
  0.0 150.4 jit_solution(5239292417352713464)
XLA Ops:
  0.0 1.4 copy.6
  1.4 1.9 %multiply_bitcast_fusion.b_ref = f32[16,256,2]{2,1,0:T(8,128)} fusion(f32[2,16,256]{0,2,1:T(8,128)S(1)} %copy.6), kind=kLoop, calls=%fused_computation | loop fusion | flops 32768 | bytes 65536 | tf_op jit(solution)/shard_map/transpose | solution.py:209
  3.3 62.1 %terms.1 = (bf16[16,128,256]{2,1,0:T(8,128)(2,1)S(1)}, f32[16,128,128]{2,1,0:T(8,128)S(1)}, bf16[16,256,256]{2,1,0:T(8,128)(2,1)S(1)}, f32[256,2048]{1,0:T(8,128)}) custom-call(f32[256,2048]{1,0:T(8,128)} %q_ref.1, f32[2,256,2048]{2,1,0:T(8,128)} %k_ref.1, f32[2,256,2048]{2,1,0:T(8,128)} %v_ref.1, f32[16,256,2]{2,1,0:T(8,128)} %multiply_bitcast_fusion.b_ref), custom_call_target="tpu_custom_call" | custom-call | tf_op jit(solution)/shard_map/terms/pallas_call | solution.py:217
  65.3 0.0 copy-start
  65.3 1.3 copy-done
  66.6 82.4 %chain.1 = f32[256,2048]{1,0:T(8,128)S(1)} custom-call(bf16[16,128,256]{2,1,0:T(8,128)(2,1)S(1)} %get-tuple-element.9.trans_ref, f32[16,128,128]{2,1,0:T(8,128)S(1)} %get-tuple-element.10.state_ref, bf16[16,256,256]{2,1,0:T(8,128)(2,1)} %copy-done, f32[256,2048]{1,0:T(8,128)} %get-tuple-element.12.inner_ref), custom_call_target="tpu_custom_call" | custom-call | tf_op jit(solution)/shard_map/chain/pallas_call | solution.py:234
  149.0 1.3 copy.10
Async XLA Ops:
  65.3 1.3 copy-start

commit v2 on v1

--- a/solution.py
+++ b/solution.py
@@ -15,6 +15,8 @@
 BF16 = jnp.bfloat16
 MESH = pl.DeviceIdType.MESH
 VMEM_LIMIT = 48 * 1024 * 1024
+PARTS = 2
+LAG = 2
 
 
 def split(x):
@@ -37,7 +39,8 @@
     return both[:, :width] + both[:, width:]
 
 
-def terms_kernel(q_ref, k_ref, v_ref, b_ref, trans_ref, state_ref, qeff_ref, inner_ref):
+def head_terms(h, q_ref, k_ref, v_ref, b_ref, trans_ref, state_ref, qeff_ref, inner_ref):
+    columns = pl.ds(pl.multiple_of(h * DK, DK), DK)
     tokens = q_ref.shape[0]
     groups = range(tokens // GROUP)
     row = lax.broadcasted_iota(jnp.int32, (SUB, SUB), 0)
@@ -54,12 +57,12 @@
     query, key_t, right, lower, masked, inverse = [], [], [], [], [], []
     for g in groups:
         rows = slice(g * GROUP, (g + 1) * GROUP)
-        q = q_ref[rows, :]
+        q = q_ref[rows, columns]
         q = q * lax.rsqrt(jnp.sum(q * q, axis=-1, keepdims=True) + 1e-06)
-        k = jnp.concatenate([k_ref[0, rows, :], k_ref[1, rows, :]], axis=0)
+        k = jnp.concatenate([k_ref[0, rows, columns], k_ref[1, rows, columns]], axis=0)
         k = k * lax.rsqrt(jnp.sum(k * k, axis=-1, keepdims=True) + 1e-06)
-        v = jnp.concatenate([v_ref[0, rows, :], v_ref[1, rows, :]], axis=0)
-        beta = jnp.concatenate([b_ref[0, rows, 0:1], b_ref[0, rows, 1:2]], axis=0)
+        v = jnp.concatenate([v_ref[0, rows, columns], v_ref[1, rows, columns]], axis=0)
+        beta = jnp.concatenate([b_ref[h, rows, 0:1], b_ref[h, rows, 1:2]], axis=0)
         kb = k * beta
         kt = k.T
         both = product(wide(jnp.concatenate([kb, q], axis=0)), tall(kt))
@@ -97,16 +100,17 @@
             pushed = pushed + moved[:SUB, DK:]
             inner = inner + moved[SUB:, DK:]
             trans, qeff = moved[:SUB, :DK], moved[SUB:, :DK]
-        qeff_ref[0, rows, :] = wide(qeff)
-        inner_ref[rows, :] = inner
+        qeff_ref[h, rows, :] = wide(qeff)
+        inner_ref[rows, columns] = inner
         prefix = jnp.concatenate([trans, pushed], axis=1)
-    trans_ref[0] = wide(trans)
-    state_ref[0] = pushed
-
-
-def chain_kernel(
-    ctx_n, head_n, width, trans_ref, state_ref, qeff_ref, inner_ref, out_ref,
-    arriving, leaving, mine, theirs, send_sem, recv_sem, sum_send, sum_recv,
+    trans_ref[h] = tall(trans.T)
+    state_ref[h] = pushed.T
+
+
+def mixer_kernel(
+    ctx_n, head_n, width, q_ref, k_ref, v_ref, b_ref, out_ref,
+    trans_ref, state_ref, qeff_ref, arriving, leaving, mine, theirs,
+    send_sem, recv_sem, sum_send, sum_recv,
 ):
     heads, tokens = qeff_ref.shape[:2]
     me = lax.axis_index("ctx")
@@ -125,44 +129,67 @@
     def _():
         pl.semaphore_signal(barrier, inc=1, device_id=(me + 1, core), device_id_type=MESH)
 
-    @pl.when(me == 0)
-    def _():
-        arriving[...] = jnp.zeros_like(arriving)
-
     neighbours = jnp.minimum(me, 1) + jnp.minimum(ctx_n - 1 - me, 1)
     pl.semaphore_wait(barrier, neighbours + (head_n - 1))
 
     mine[...] = jnp.zeros_like(mine)
-
-    def copy_of(h, target):
+    part = DV // PARTS
+
+    def copy_of(h, c, target):
+        rows = pl.ds(c * part, part)
         return pltpu.make_async_remote_copy(
-            src_ref=leaving.at[h],
-            dst_ref=arriving.at[h],
-            send_sem=send_sem.at[h],
-            recv_sem=recv_sem.at[h],
+            src_ref=leaving.at[h, rows],
+            dst_ref=arriving.at[h, rows],
+            send_sem=send_sem.at[h, c],
+            recv_sem=recv_sem.at[h, c],
             device_id=(target, core),
             device_id_type=MESH,
         )
 
-    def one_head(h, carry):
+    def relay_head(h):
+        for c in range(PARTS):
+            rows = pl.ds(c * part, part)
+
+            @pl.when(me == 0)
+            def _():
+                leaving[h, rows] = state_ref[h, rows]
+
+            @pl.when(me > 0)
+            def _():
+                copy_of(h, c, me).wait_recv()
+                leaving[h, rows] = (
+                    product(wide(arriving[h, rows]), trans_ref[h]) + state_ref[h, rows]
+                )
+
+            @pl.when(me < ctx_n - 1)
+            def _():
+                copy_of(h, c, me + 1).start()
+
+        columns = pl.ds(pl.multiple_of(h * DV, DV), DV)
+
         @pl.when(me > 0)
         def _():
-            copy_of(h, me).wait_recv()
-
-        state = tall(arriving[h])
-
-        @pl.when(me < ctx_n - 1)
+            out_ref[:, columns] += product(qeff_ref[h], tall(arriving[h].T))
+
+        read = out_ref[:, columns]
+        mine[...] += read * read
+
+    lag = jnp.minimum(LAG * me, heads)
+
+    def step(i, carry):
+        @pl.when(i < heads)
         def _():
-            leaving[h] = product(trans_ref[h], state) + state_ref[h]
-            copy_of(h, me + 1).start()
-
-        columns = pl.ds(pl.multiple_of(h * DV, DV), DV)
-        read = product(qeff_ref[h], state) + inner_ref[:, columns]
-        out_ref[:, columns] = read
-        mine[...] += read * read
+            head_terms(
+                i, q_ref, k_ref, v_ref, b_ref, trans_ref, state_ref, qeff_ref, out_ref
+            )
+
+        @pl.when(i >= lag)
+        def _():
+            relay_head(i - lag)
+
         return carry
 
-    lax.fori_loop(0, heads, one_head, 0)
+    lax.fori_loop(0, heads + lag, step, 0)
 
     def sum_copy(off):
         return pltpu.make_async_remote_copy(
@@ -195,7 +222,8 @@
     @pl.when(me < ctx_n - 1)
     def _():
         def finish(h, carry):
-            copy_of(h, me + 1).wait_send()
+            for c in range(PARTS):
+                copy_of(h, c, me + 1).wait_send()
             return carry
 
         lax.fori_loop(0, heads, finish, 0)
@@ -208,49 +236,31 @@
     head_n = lax.axis_size("head")
     beta = (2.0 * jax.nn.sigmoid(beta_logit)).transpose(1, 2, 0)
     shape = jax.ShapeDtypeStruct
-    rows_of = pl.BlockSpec((tokens, DK), lambda h: (0, h))
-    pair_of = pl.BlockSpec((2, tokens, DK), lambda h: (0, 0, h))
-
-    def head_of(*block):
-        return pl.BlockSpec((1,) + block, lambda h: (h, 0, 0))
-
-    trans, state, qeff, inner = pl.pallas_call(
-        terms_kernel,
-        grid=(heads,),
-        in_specs=[rows_of, pair_of, pair_of, head_of(tokens, 2)],
-        out_specs=[head_of(DK, 2 * DK), head_of(DK, DV), head_of(tokens, 2 * DK), rows_of],
-        out_shape=[
-            shape((heads, DK, 2 * DK), BF16),
-            shape((heads, DK, DV), F32),
-            shape((heads, tokens, 2 * DK), BF16),
-            shape((tokens, heads * DV), F32),
-        ],
-        compiler_params=pltpu.CompilerParams(vmem_limit_bytes=VMEM_LIMIT),
-        name="terms",
-    )(query_rows, key_rows, reflection_value_rows, beta)
-
     whole = pl.BlockSpec(memory_space=pltpu.VMEM)
     width = float(head_n * heads * DV)
     return pl.pallas_call(
-        functools.partial(chain_kernel, ctx_n, head_n, width),
+        functools.partial(mixer_kernel, ctx_n, head_n, width),
         in_specs=[whole] * 4,
         out_specs=whole,
         out_shape=shape((tokens, heads * DV), F32),
         scratch_shapes=[
-            pltpu.VMEM((heads, DK, DV), F32),
-            pltpu.VMEM((heads, DK, DV), F32),
+            pltpu.VMEM((heads, 2 * DK, 2 * DK), BF16),
+            pltpu.VMEM((heads, DV, DK), F32),
+            pltpu.VMEM((heads, tokens, 2 * DK), BF16),
+            pltpu.VMEM((heads, DV, DK), F32),
+            pltpu.VMEM((heads, DV, DK), F32),
             pltpu.VMEM((tokens, DV), F32),
             pltpu.VMEM((max(head_n - 1, 1), tokens, DV), F32),
-            pltpu.SemaphoreType.DMA((heads,)),
-            pltpu.SemaphoreType.DMA((heads,)),
+            pltpu.SemaphoreType.DMA((heads, PARTS)),
+            pltpu.SemaphoreType.DMA((heads, PARTS)),
             pltpu.SemaphoreType.DMA((max(head_n - 1, 1),)),
             pltpu.SemaphoreType.DMA((max(head_n - 1, 1),)),
         ],
         compiler_params=pltpu.CompilerParams(
             collective_id=0, has_side_effects=True, vmem_limit_bytes=VMEM_LIMIT
         ),
-        name="chain",
-    )(trans, state, qeff, inner)
+        name="mixer",
+    )(query_rows, key_rows, reflection_value_rows, beta)
 
 
 def solution(mesh):

time: 151 us -> 131 us (0.87)
  Pallas kernels: 144 us -> 126 us
    pallas_call x2 -> x1, Pallas kernels: 144 us -> 126 us  [local(): pl.pallas_call(functools.partial(mixer_kernel, ctx_n, head_n, width), in_...]
where the time goes in v2:
time: 131 us; the launch traced here: 130 us
  Pallas kernels  126 us (96%)
  local copies, waits for them, and re-layouts  2.71 us (2%)
  other arithmetic  1.87 us (1%)
    pallas_call x1, Pallas kernels, local(): pl.pallas_call(functools.partial(mixer_kernel, ctx_n, head_n, width), in_...  126 us
    unnamed x4, local copies, waits for them, and re-layouts  2.71 us

profile of v2, /device:TPU:31, one launch (start us, length us, event | category | flops | bytes accessed | tf_op | source)
XLA Modules:
  0.0 130.3 jit_solution(9506885241743867189)
XLA Ops:
  0.0 1.4 %copy.6 = f32[2,16,256]{0,2,1:T(8,128)S(1)} copy(f32[2,16,256]{2,1,0:T(8,128)} %param.7) | data formatting | bytes 65536 | tf_op args[3]
  1.4 0.0 copy-start
  1.4 1.9 %multiply_bitcast_fusion.b_ref = f32[16,256,2]{2,1,0:T(8,128)} fusion(f32[2,16,256]{0,2,1:T(8,128)S(1)} %copy.6), kind=kLoop, calls=%fused_computation | loop fusion | flops 32768 | bytes 65536 | tf_op jit(solution)/shard_map/transpose | solution.py:237
  3.3 0.0 copy-done
  3.3 125.7 %mixer.1 = f32[256,2048]{1,0:T(8,128)S(1)} custom-call(f32[256,2048]{1,0:T(8,128)S(1)} %copy-done, f32[2,256,2048]{2,1,0:T(8,128)} %k_ref.1, f32[2,256,2048]{2,1,0:T(8,128)} %v_ref.1, f32[16,256,2]{2,1,0:T(8,128)} %multiply_bitcast_fusion.b_ref), custom_call_target="tpu_custom_call" | custom-call | tf_op jit(solution)/shard_map/mixer/pallas_call | solution.py:241
  129.0 1.3 %copy.10 = f32[256,2048]{1,0:T(8,128)} copy(f32[256,2048]{1,0:T(8,128)S(1)} %mixer.1) | data formatting | bytes 4194304
Async XLA Ops:
  1.4 1.9 %copy-start = (f32[256,2048]{1,0:T(8,128)S(1)}, f32[256,2048]{1,0:T(8,128)}, u32[]{:S(2)}) copy-start(f32[256,2048]{1,0:T(8,128)} %q_ref.1) | copy-start | bytes 6291460

commit v3 on v2

--- a/solution.py
+++ b/solution.py
@@ -16,7 +16,7 @@
 MESH = pl.DeviceIdType.MESH
 VMEM_LIMIT = 48 * 1024 * 1024
 PARTS = 2
-LAG = 2
+TEAM = 4
 
 
 def split(x):
@@ -39,7 +39,7 @@
     return both[:, :width] + both[:, width:]
 
 
-def head_terms(h, q_ref, k_ref, v_ref, b_ref, trans_ref, state_ref, qeff_ref, inner_ref):
+def head_terms(h, q_ref, k_ref, v_ref, b_ref, trans_ref, own_ref, qeff_ref, inner_ref):
     columns = pl.ds(pl.multiple_of(h * DK, DK), DK)
     tokens = q_ref.shape[0]
     groups = range(tokens // GROUP)
@@ -103,93 +103,177 @@
         qeff_ref[h, rows, :] = wide(qeff)
         inner_ref[rows, columns] = inner
         prefix = jnp.concatenate([trans, pushed], axis=1)
-    trans_ref[h] = tall(trans.T)
-    state_ref[h] = pushed.T
+    trans_t = trans.T
+    trans_ref[h] = tall(trans_t)
+    own_ref[h] = jnp.concatenate([trans_t, pushed.T], axis=0)
 
 
 def mixer_kernel(
     ctx_n, head_n, width, q_ref, k_ref, v_ref, b_ref, out_ref,
-    trans_ref, state_ref, qeff_ref, arriving, leaving, mine, theirs,
-    send_sem, recv_sem, sum_send, sum_recv,
+    trans_ref, own_ref, qeff_ref, before, after, state_in, state_out, mine, theirs,
+    pair_send, pair_recv, state_send, state_recv, spread_send, sum_send, sum_recv,
 ):
     heads, tokens = qeff_ref.shape[:2]
     me = lax.axis_index("ctx")
     core = lax.axis_index("head")
     peers = [lax.rem(core + off, head_n) for off in range(1, head_n)]
+    inner_n = TEAM if ctx_n % TEAM == 0 else 1
+    outer_n = ctx_n // inner_n
+    last = inner_n - 1
+    team, rank = me // inner_n, lax.rem(me, inner_n)
+    mates = [team * inner_n + lax.rem(rank + off, inner_n) for off in range(1, inner_n)]
 
     barrier = pltpu.get_barrier_semaphore()
+
+    def greet(ctx, head):
+        pl.semaphore_signal(barrier, inc=1, device_id=(ctx, head), device_id_type=MESH)
+
     for peer in peers:
-        pl.semaphore_signal(barrier, inc=1, device_id=(me, peer), device_id_type=MESH)
-
-    @pl.when(me > 0)
+        greet(me, peer)
+    for mate in mates:
+        greet(mate, core)
+
+    @pl.when((rank == last) & (team > 0))
     def _():
-        pl.semaphore_signal(barrier, inc=1, device_id=(me - 1, core), device_id_type=MESH)
-
-    @pl.when(me < ctx_n - 1)
+        greet(me - inner_n, core)
+
+    @pl.when((rank == last) & (team < outer_n - 1))
     def _():
-        pl.semaphore_signal(barrier, inc=1, device_id=(me + 1, core), device_id_type=MESH)
-
-    neighbours = jnp.minimum(me, 1) + jnp.minimum(ctx_n - 1 - me, 1)
-    pl.semaphore_wait(barrier, neighbours + (head_n - 1))
+        greet(me + inner_n, core)
+
+    is_last = 1 - jnp.minimum(last - rank, 1)
+    beyond = jnp.minimum(team, 1) + jnp.minimum(outer_n - 1 - team, 1)
+    pl.semaphore_wait(barrier, is_last * beyond + (head_n - 1 + inner_n - 1))
 
     mine[...] = jnp.zeros_like(mine)
     part = DV // PARTS
 
-    def copy_of(h, c, target):
+    def pair_copy(h, c):
+        rows = pl.ds(c * DK, DK)
+        return pltpu.make_async_remote_copy(
+            src_ref=after.at[h, rows],
+            dst_ref=before.at[h, rows],
+            send_sem=pair_send.at[h, c],
+            recv_sem=pair_recv.at[h, c],
+            device_id=(me + 1, core),
+            device_id_type=MESH,
+        )
+
+    def state_copy(h, c):
         rows = pl.ds(c * part, part)
         return pltpu.make_async_remote_copy(
-            src_ref=leaving.at[h, rows],
-            dst_ref=arriving.at[h, rows],
-            send_sem=send_sem.at[h, c],
-            recv_sem=recv_sem.at[h, c],
-            device_id=(target, core),
+            src_ref=state_out.at[h, rows],
+            dst_ref=state_in.at[h, rows],
+            send_sem=state_send.at[h, c],
+            recv_sem=state_recv.at[h, c],
+            device_id=(me + inner_n, core),
             device_id_type=MESH,
         )
+
+    def spread_copy(h, c, mate):
+        rows = pl.ds(c * part, part)
+        return pltpu.make_async_remote_copy(
+            src_ref=state_in.at[h, rows],
+            dst_ref=state_in.at[h, rows],
+            send_sem=spread_send.at[h, c, mate],
+            recv_sem=state_recv.at[h, c],
+            device_id=(mates[mate], core),
+            device_id_type=MESH,
+        )
+
+    def compose_head(h):
+        for c in range(2):
+            rows = pl.ds(c * DK, DK)
+
+            @pl.when(rank == 0)
+            def _():
+                after[h, rows] = own_ref[h, rows]
+
+            @pl.when(rank > 0)
+            def _():
+                pair_copy(h, c).wait_recv()
+                moved = product(wide(before[h, rows]), trans_ref[h])
+                after[h, rows] = moved if c == 0 else moved + own_ref[h, rows]
+
+            @pl.when(rank < last)
+            def _():
+                pair_copy(h, c).start()
 
     def relay_head(h):
         for c in range(PARTS):
             rows = pl.ds(c * part, part)
-
-            @pl.when(me == 0)
-            def _():
-                leaving[h, rows] = state_ref[h, rows]
-
-            @pl.when(me > 0)
-            def _():
-                copy_of(h, c, me).wait_recv()
-                leaving[h, rows] = (
-                    product(wide(arriving[h, rows]), trans_ref[h]) + state_ref[h, rows]
+            shifted = pl.ds(DK + c * part, part)
+
+            @pl.when(team > 0)
+            def _():
+                state_copy(h, c).wait_recv()
+
+            @pl.when((team > 0) & (team < outer_n - 1))
+            def _():
+                state_out[h, rows] = (
+                    product(wide(state_in[h, rows]), tall(after[h, :DK])) + after[h, shifted]
                 )
 
-            @pl.when(me < ctx_n - 1)
-            def _():
-                copy_of(h, c, me + 1).start()
-
+            @pl.when(team == 0)
+            def _():
+                state_out[h, rows] = after[h, shifted]
+
+            @pl.when(team < outer_n - 1)
+            def _():
+                state_copy(h, c).start()
+
+            @pl.when(team > 0)
+            def _():
+                for mate in range(inner_n - 1):
+                    spread_copy(h, c, mate).start()
+
+    def read_head(h):
         columns = pl.ds(pl.multiple_of(h * DV, DV), DV)
 
-        @pl.when(me > 0)
-        def _():
-            out_ref[:, columns] += product(qeff_ref[h], tall(arriving[h].T))
+        @pl.when((rank < last) & (team > 0))
+        def _():
+            for c in range(PARTS):
+                state_copy(h, c).wait_recv()
+
+        @pl.when((rank == 0) & (team > 0))
+        def _():
+            out_ref[:, columns] += product(qeff_ref[h], tall(state_in[h].T))
+
+        @pl.when((rank > 0) & (team == 0))
+        def _():
+            out_ref[:, columns] += product(qeff_ref[h], tall(before[h, DK:].T))
+
+        @pl.when((rank > 0) & (team > 0))
+        def _():
+            state = product(wide(state_in[h]), tall(before[h, :DK])) + before[h, DK:]
+            out_ref[:, columns] += product(qeff_ref[h], tall(state.T))
 
         read = out_ref[:, columns]
         mine[...] += read * read
 
-    lag = jnp.minimum(LAG * me, heads)
+    relay_lag = last + team
+    read_lag = jnp.maximum(heads, relay_lag + 1)
 
     def step(i, carry):
         @pl.when(i < heads)
         def _():
-            head_terms(
-                i, q_ref, k_ref, v_ref, b_ref, trans_ref, state_ref, qeff_ref, out_ref
-            )
-
-        @pl.when(i >= lag)
-        def _():
-            relay_head(i - lag)
+            head_terms(i, q_ref, k_ref, v_ref, b_ref, trans_ref, own_ref, qeff_ref, out_ref)
+
+        @pl.when((i >= rank) & (i < heads + rank))
+        def _():
+            compose_head(i - rank)
+
+        @pl.when((rank == last) & (i >= relay_lag) & (i < heads + relay_lag))
+        def _():
+            relay_head(i - relay_lag)
+
+        @pl.when(i >= read_lag)
+        def _():
+            read_head(i - read_lag)
 
         return carry
 
-    lax.fori_loop(0, heads + lag, step, 0)
+    lax.fori_loop(0, heads + read_lag, step, 0)
 
     def sum_copy(off):
         return pltpu.make_async_remote_copy(
@@ -219,14 +303,26 @@
 
     lax.fori_loop(0, heads, scale_head, 0)
 
-    @pl.when(me < ctx_n - 1)
-    def _():
-        def finish(h, carry):
+    def finish(h, carry):
+        @pl.when(rank < last)
+        def _():
+            for c in range(2):
+                pair_copy(h, c).wait_send()
+
+        @pl.when((rank == last) & (team < outer_n - 1))
+        def _():
             for c in range(PARTS):
-                copy_of(h, c, me + 1).wait_send()
-            return carry
-
-        lax.fori_loop(0, heads, finish, 0)
+                state_copy(h, c).wait_send()
+
+        @pl.when((rank == last) & (team > 0))
+        def _():
+            for c in range(PARTS):
+                for mate in range(inner_n - 1):
+                    spread_copy(h, c, mate).wait_send()
+
+        return carry
+
+    lax.fori_loop(0, heads, finish, 0)
 
 
 def local(query_rows, key_rows, reflection_value_rows, beta_logit):
@@ -245,14 +341,19 @@
         out_shape=shape((tokens, heads * DV), F32),
         scratch_shapes=[
             pltpu.VMEM((heads, 2 * DK, 2 * DK), BF16),
-            pltpu.VMEM((heads, DV, DK), F32),
+            pltpu.VMEM((heads, DK + DV, DK), F32),
             pltpu.VMEM((heads, tokens, 2 * DK), BF16),
+            pltpu.VMEM((heads, DK + DV, DK), F32),
+            pltpu.VMEM((heads, DK + DV, DK), F32),
             pltpu.VMEM((heads, DV, DK), F32),
             pltpu.VMEM((heads, DV, DK), F32),
             pltpu.VMEM((tokens, DV), F32),
             pltpu.VMEM((max(head_n - 1, 1), tokens, DV), F32),
+            pltpu.SemaphoreType.DMA((heads, 2)),
+            pltpu.SemaphoreType.DMA((heads, 2)),
             pltpu.SemaphoreType.DMA((heads, PARTS)),
             pltpu.SemaphoreType.DMA((heads, PARTS)),
+            pltpu.SemaphoreType.DMA((heads, PARTS, TEAM)),
             pltpu.SemaphoreType.DMA((max(head_n - 1, 1),)),
             pltpu.SemaphoreType.DMA((max(head_n - 1, 1),)),
         ],

time: 131 us -> 106 us (0.81)
  Pallas kernels: 126 us -> 101 us
    pallas_call x1, Pallas kernels: 126 us -> 101 us  [local(): pl.pallas_call(functools.partial(mixer_kernel, ctx_n, head_n, width), in_...]
where the time goes in v3:
time: 106 us; the launch traced here: 105 us
  Pallas kernels  101 us (95%)
  local copies, waits for them, and re-layouts  2.71 us (3%)
  other arithmetic  1.87 us (2%)
    pallas_call x1, Pallas kernels, local(): pl.pallas_call(functools.partial(mixer_kernel, ctx_n, head_n, width), in_...  101 us
    unnamed x4, local copies, waits for them, and re-layouts  2.71 us

profile of v3, /device:TPU:31, one launch (start us, length us, event | category | flops | bytes accessed | tf_op | source)
XLA Modules:
  0.0 105.4 jit_solution(9200844988066779661)
XLA Ops:
  0.0 1.4 %copy.6 = f32[2,16,256]{0,2,1:T(8,128)S(1)} copy(f32[2,16,256]{2,1,0:T(8,128)} %param.7) | data formatting | bytes 65536 | tf_op args[3]
  1.4 0.0 copy-start
  1.4 1.9 %multiply_bitcast_fusion.b_ref = f32[16,256,2]{2,1,0:T(8,128)} fusion(f32[2,16,256]{0,2,1:T(8,128)S(1)} %copy.6), kind=kLoop, calls=%fused_computation | loop fusion | flops 32768 | bytes 65536 | tf_op jit(solution)/shard_map/transpose | solution.py:333
  3.3 0.0 copy-done
  3.3 100.8 %mixer.1 = f32[256,2048]{1,0:T(8,128)S(1)} custom-call(f32[256,2048]{1,0:T(8,128)S(1)} %copy-done, f32[2,256,2048]{2,1,0:T(8,128)} %k_ref.1, f32[2,256,2048]{2,1,0:T(8,128)} %v_ref.1, f32[16,256,2]{2,1,0:T(8,128)} %multiply_bitcast_fusion.b_ref), custom_call_target="tpu_custom_call" | custom-call | tf_op jit(solution)/shard_map/mixer/pallas_call | solution.py:337
  104.1 1.3 %copy.10 = f32[256,2048]{1,0:T(8,128)} copy(f32[256,2048]{1,0:T(8,128)S(1)} %mixer.1) | data formatting | bytes 4194304
Async XLA Ops:
  1.4 1.9 %copy-start = (f32[256,2048]{1,0:T(8,128)S(1)}, f32[256,2048]{1,0:T(8,128)}, u32[]{:S(2)}) copy-start(f32[256,2048]{1,0:T(8,128)} %q_ref.1) | copy-start | bytes 6291460

commit v4 on v3

--- a/solution.py
+++ b/solution.py
@@ -39,10 +39,10 @@
     return both[:, :width] + both[:, width:]
 
 
-def head_terms(h, q_ref, k_ref, v_ref, b_ref, trans_ref, own_ref, qeff_ref, inner_ref):
-    columns = pl.ds(pl.multiple_of(h * DK, DK), DK)
+def heads_terms(first, count, q_ref, k_ref, v_ref, b_ref, trans_ref, own_ref, qeff_ref, inner_ref):
     tokens = q_ref.shape[0]
-    groups = range(tokens // GROUP)
+    per_head = tokens // GROUP
+    groups = range(count * per_head)
     row = lax.broadcasted_iota(jnp.int32, (SUB, SUB), 0)
     col = lax.broadcasted_iota(jnp.int32, (SUB, SUB), 1)
     row_order = 2 * (row % GROUP) + row // GROUP
@@ -54,15 +54,24 @@
     key_token = lax.broadcasted_iota(jnp.int32, (GROUP, SUB), 1) % GROUP
     visible = key_token <= token
 
+    betas = jnp.concatenate(
+        [jnp.broadcast_to(b_ref[j, pl.ds(first + u, 1), :], (8, tokens)) for u in range(count) for j in range(2)],
+        axis=0,
+    )
+    betas = (2.0 / (1.0 + jnp.exp(-betas))).T
+
     query, key_t, right, lower, masked, inverse = [], [], [], [], [], []
     for g in groups:
-        rows = slice(g * GROUP, (g + 1) * GROUP)
+        h = first + g // per_head
+        columns = pl.ds(pl.multiple_of(h * DK, DK), DK)
+        rows = slice(g % per_head * GROUP, (g % per_head + 1) * GROUP)
         q = q_ref[rows, columns]
         q = q * lax.rsqrt(jnp.sum(q * q, axis=-1, keepdims=True) + 1e-06)
         k = jnp.concatenate([k_ref[0, rows, columns], k_ref[1, rows, columns]], axis=0)
         k = k * lax.rsqrt(jnp.sum(k * k, axis=-1, keepdims=True) + 1e-06)
         v = jnp.concatenate([v_ref[0, rows, columns], v_ref[1, rows, columns]], axis=0)
-        beta = jnp.concatenate([b_ref[h, rows, 0:1], b_ref[h, rows, 1:2]], axis=0)
+        c = 16 * (g // per_head)
+        beta = jnp.concatenate([betas[rows, c : c + 1], betas[rows, c + 8 : c + 9]], axis=0)
         kb = k * beta
         kt = k.T
         both = product(wide(jnp.concatenate([kb, q], axis=0)), tall(kt))
@@ -92,10 +101,12 @@
     ]
     prefix = None
     for g in groups:
-        rows = slice(g * GROUP, (g + 1) * GROUP)
+        h = first + g // per_head
+        columns = pl.ds(pl.multiple_of(h * DK, DK), DK)
+        rows = slice(g % per_head * GROUP, (g % per_head + 1) * GROUP)
         pushed, inner = terms[g][:SUB, :DV], terms[g][SUB:, :DV]
         trans, qeff = eye - terms[g][:SUB, DV:], query[g] - terms[g][SUB:, DV:]
-        if prefix is not None:
+        if g % per_head:
             moved = product(wide(jnp.concatenate([trans, qeff], axis=0)), tall(prefix))
             pushed = pushed + moved[:SUB, DK:]
             inner = inner + moved[SUB:, DK:]
@@ -103,9 +114,10 @@
         qeff_ref[h, rows, :] = wide(qeff)
         inner_ref[rows, columns] = inner
         prefix = jnp.concatenate([trans, pushed], axis=1)
-    trans_t = trans.T
-    trans_ref[h] = tall(trans_t)
-    own_ref[h] = jnp.concatenate([trans_t, pushed.T], axis=0)
+        if g % per_head == per_head - 1:
+            trans_t = trans.T
+            trans_ref[h] = tall(trans_t)
+            own_ref[h] = jnp.concatenate([trans_t, pushed.T], axis=0)
 
 
 def mixer_kernel(
@@ -254,10 +266,12 @@
     relay_lag = last + team
     read_lag = jnp.maximum(heads, relay_lag + 1)
 
+    at_once = 2 if heads % 2 == 0 else 1
+
     def step(i, carry):
-        @pl.when(i < heads)
-        def _():
-            head_terms(i, q_ref, k_ref, v_ref, b_ref, trans_ref, own_ref, qeff_ref, out_ref)
+        @pl.when((i < heads) & (lax.rem(i, at_once) == 0))
+        def _():
+            heads_terms(i, at_once, q_ref, k_ref, v_ref, b_ref, trans_ref, own_ref, qeff_ref, out_ref)
 
         @pl.when((i >= rank) & (i < heads + rank))
         def _():
@@ -330,7 +344,6 @@
     heads = query_rows.shape[1] // DK
     ctx_n = lax.axis_size("ctx")
     head_n = lax.axis_size("head")
-    beta = (2.0 * jax.nn.sigmoid(beta_logit)).transpose(1, 2, 0)
     shape = jax.ShapeDtypeStruct
     whole = pl.BlockSpec(memory_space=pltpu.VMEM)
     width = float(head_n * heads * DV)
@@ -361,7 +374,7 @@
             collective_id=0, has_side_effects=True, vmem_limit_bytes=VMEM_LIMIT
         ),
         name="mixer",
-    )(query_rows, key_rows, reflection_value_rows, beta)
+    )(query_rows, key_rows, reflection_value_rows, beta_logit)
 
 
 def solution(mesh):

time: 106 us -> 103 us (0.972)
  the two profiles are of different devices: /device:TPU:31 before, /device:TPU:25 now
where the time goes in v4:
time: 103 us
  Pallas kernels  99.2 us (96%)
  local copies, waits for them, and re-layouts  3.67 us (4%)
    pallas_call x1, Pallas kernels, local(): pl.pallas_call(functools.partial(mixer_kernel, ctx_n, head_n, width), in_...  99.2 us
    unnamed x5, local copies, waits for them, and re-layouts  3.67 us

profile of v4, /device:TPU:25, one launch (start us, length us, event | category | flops | bytes accessed | tf_op | source)
XLA Modules:
  0.0 102.9 jit_solution(14281224326928933546)
XLA Ops:
  0.0 0.0 copy-start
  0.0 1.6 %copy-done = f32[256,2048]{1,0:T(8,128)S(1)} copy-done((f32[256,2048]{1,0:T(8,128)S(1)}, f32[256,2048]{1,0:T(8,128)}, u32[]{:S(2)}) %copy-start) | copy-done | bytes 2097176
  1.6 0.0 copy-start.1
  1.6 0.8 copy-done.1
  2.4 99.2 %mixer.1 = f32[256,2048]{1,0:T(8,128)S(1)} custom-call(f32[256,2048]{1,0:T(8,128)S(1)} %copy-done, f32[2,256,2048]{2,1,0:T(8,128)} %k_ref.1, f32[2,256,2048]{2,1,0:T(8,128)} %v_ref.1, f32[2,16,256]{2,1,0:T(8,128)S(1)} %copy-done.1), custom_call_target="tpu_custom_call" | custom-call | tf_op jit(solution)/shard_map/mixer/pallas_call | solution.py:350
  101.6 1.3 %copy.6 = f32[256,2048]{1,0:T(8,128)} copy(f32[256,2048]{1,0:T(8,128)S(1)} %mixer.1) | data formatting | bytes 4194304
Async XLA Ops:
  0.0 1.6 %copy-start = (f32[256,2048]{1,0:T(8,128)S(1)}, f32[256,2048]{1,0:T(8,128)}, u32[]{:S(2)}) copy-start(f32[256,2048]{1,0:T(8,128)} %q_ref.1) | copy-start | bytes 6291460
  1.6 0.8 copy-start.1
